TPU v7x, 256 devices: a whole 4x4x8 slice. The times are simulated.
256 devices in a mesh: cores: 2 (over core), row: 16 (over y, x), vec: 8 (over z).
Axes of the slice: x: 4, y: 4, z: 8, core: 2. Of those that a mesh axis runs over, the one named last changes fastest.
Arguments:
- train_cores: float32 [8, 512, 256, 256], P('vec', 'cores', 'row'), may hold values from -0.01953125 to 0.01953125
- sketch: float32 [512, 128], P('cores'), may hold values from -6 to 6
- exit_sketch: float32 [256, 128], replicated, may hold values from -6 to 6
Outputs:
- rounded: float32 [8, 256, 256, 128], P('vec', 'cores', 'row')
- interface_bases: float32 [8, 512, 128], P('vec', 'cores')
- margins: float32 [8, 256, 1024], P('vec', 'cores')
All inputs are finite; a program needn't handle non-finite values.
Results may differ from a plain program's by a relative error of at most 0.0003.
Values sent between devices are 32-bit elements; how exact they have to be, the bound alone decides.
A program may use at most 128 MiB of HBM per device.

v0:
```python
import math

import jax
import jax.numpy as jnp
from jax import lax
from jax.sharding import PartitionSpec as P

MODE = 256


def broadcast(block, axis, holder):
    block = jnp.where(lax.axis_index(axis) == holder, block, jnp.zeros_like(block))
    return lax.psum(block, axis)


def product(left_mat, right_mat):
    return jnp.dot(
        left_mat, right_mat, precision=lax.Precision.HIGHEST, preferred_element_type=jnp.float32
    )


def orthonormal(gram_matrix, sketch):
    powered = product(gram_matrix, product(gram_matrix, sketch))
    chol_low = jnp.linalg.cholesky(product(powered.T, powered))
    return jax.scipy.linalg.solve_triangular(chol_low, powered.T, lower=True).T


def local(train_cores, sketch, exit_sketch):
    block_core = train_cores[0]
    full_rank = block_core.shape[0]
    mode_count = block_core.shape[1]
    kept_rank = sketch.shape[1]
    chain_len = lax.axis_size("cores")
    position = lax.axis_index("cores")
    vector_count = lax.axis_size("vec")
    identity = jnp.eye(full_rank, dtype=jnp.float32)
    zero_square = jnp.zeros((full_rank, full_rank), jnp.float32)
    row_major = block_core.reshape(full_rank * mode_count, full_rank)
    wide_core = block_core.reshape(full_rank, mode_count * full_rank)

    def forward_gram(lower_in):
        absorbed = product(lower_in.T, wide_core).reshape(full_rank * mode_count, full_rank)
        return product(absorbed.T, absorbed)

    def zero_gram(operand):
        return zero_square

    lower_prev = identity
    lower_own = identity
    gram_own = identity
    for link_index in range(chain_len):
        active = position == link_index
        partial_value = lax.cond(active, forward_gram, zero_gram, lower_prev)
        summed = jnp.where(active, lax.psum(partial_value, "row"), identity)
        factor = jnp.linalg.cholesky(summed)
        if link_index + 1 < chain_len:
            arrived = broadcast(factor, "cores", link_index)
            lower_prev = jnp.where(position == link_index + 1, arrived, lower_prev)
        lower_own = jnp.where(active, factor, lower_own)
        gram_own = jnp.where(active, summed, gram_own)
    is_last = position == chain_len - 1
    incoming = orthonormal(gram_own, exit_sketch)

    def right_map_of(incoming_frame):
        solved = jax.scipy.linalg.solve_triangular(lower_own, incoming_frame, lower=True, trans=1)
        return jnp.where(is_last, incoming_frame, solved)

    def backward_gram(incoming_frame):
        reduced = product(row_major, right_map_of(incoming_frame)).reshape(
            full_rank, mode_count * kept_rank
        )
        mixed_core = product(lower_prev.T, reduced)
        return product(mixed_core, mixed_core.T)

    frame_own = jnp.zeros((full_rank, kept_rank), jnp.float32)
    for link_index in range(chain_len):
        target = chain_len - 1 - link_index
        active = position == target
        partial_value = lax.cond(active, backward_gram, zero_gram, incoming)
        summed = jnp.where(active, lax.psum(partial_value, "row"), identity)
        frame = orthonormal(summed, sketch)
        if target > 0:
            arrived = broadcast(frame, "cores", target)
            incoming = jnp.where(position == target - 1, arrived, incoming)
        frame_own = jnp.where(active, frame, frame_own)
    reduced = product(row_major, right_map_of(incoming)).reshape(full_rank, mode_count * kept_rank)
    front_map = product(frame_own.T, lower_prev.T)
    shaped = product(front_map, reduced)
    rounded = (shaped * math.sqrt(kept_rank * MODE)).reshape(1, kept_rank, mode_count, kept_rank)
    bases_out = (frame_own * math.sqrt(full_rank))[None]
    gathered, frames_all = (
        lax.all_gather(shaped[None], "vec", axis=0, tiled=True),
        lax.all_gather(frame_own[None], "vec", axis=0, tiled=True),
    )
    start_env = jnp.einsum("az,qay->qzy", frame_own, frames_all, precision=lax.Precision.HIGHEST)
    mine_rows = shaped.reshape(kept_rank * mode_count, kept_rank)
    zero_env = jnp.zeros((vector_count, kept_rank, kept_rank), jnp.float32)

    def margin_terms(env_in):
        carried = jnp.einsum("qzw,qwx->qzx", env_in, gathered, precision=lax.Precision.HIGHEST)
        carried = carried.reshape(vector_count, kept_rank * mode_count, kept_rank)
        return jnp.einsum("cb,qcy->qby", mine_rows, carried, precision=lax.Precision.HIGHEST)

    def zero_margin(operand):
        return zero_env

    env_in = start_env
    env_own = zero_env
    for link_index in range(chain_len):
        active = position == link_index
        partial_value = lax.cond(active, margin_terms, zero_margin, env_in)
        summed = lax.psum(partial_value, "row")
        if link_index + 1 < chain_len:
            arrived = broadcast(summed, "cores", link_index)
            env_in = jnp.where(position == link_index + 1, arrived, env_in)
        env_own = jnp.where(active, summed, env_own)
    margins = env_own.transpose(1, 0, 2).reshape(kept_rank, vector_count * kept_rank)[None]
    return (rounded, bases_out, margins)


def solution(mesh):
    return jax.shard_map(
        local,
        mesh=mesh,
        in_specs=(P("vec", "cores", "row", None), P("cores", None), P()),
        out_specs=(
            P("vec", "cores", "row", None),
            P("vec", "cores", None),
            P("vec", "cores", None),
        ),
        check_vma=False,
    )
```

profile of v0, /device:TPU:1, one launch (start us, length us, event | category | flops | bytes accessed | tf_op | source)
XLA Modules:
  0.0 1188.9 jit_solution(5875113720510303117)
XLA Ops:
  16.1 11.9 all-reduce.13.cloned.1.call-start
  27.9 108.0 %all-reduce.11.cloned.1.call-done = f32[256,256]{0,1:T(8,128)} async-done(((f32[256,256]{0,1:T(8,128)}), f32[256,256]{0,1:T(8,128)}) %all-reduce.11.cloned.1.call-update) | async-done | bytes 262160 | tf_op jit(solution)/shard_map/psum | solution.py:54
  136.2 11.7 cholesky.187
  158.4 11.7 cholesky.204
  173.1 32.5 %all-reduce.13.cloned.1.call-done = f32[256,256]{0,1:T(8,128)} async-done(((f32[256,256]{0,1:T(8,128)}), f32[256,256]{0,1:T(8,128)}) %all-reduce.13.cloned.1.call-update) | async-done | bytes 262160 | tf_op jit(solution)/shard_map/psum | solution.py:13
  206.6 23.0 %conditional.7 = (f32[256,256]{1,0:T(8,128)S(1)}) conditional(s32[]{:T(128)} %convert_element_type.28, () %tuple.49, (f32[256,256]{0,1:T(8,128)S(1)}, f32[256,4096]{1,0:T(8,128)}) %tuple.170), branch_computations={%region_8.10_spmd, %region_9.11_spmd} | conditional | flops 6442450944 | bytes 21495816 | solution.py:53
  230.7 93.5 %all-reduce.15.cloned.1.call-done = f32[256,256]{0,1:T(8,128)} async-done(((f32[256,256]{0,1:T(8,128)}), f32[256,256]{0,1:T(8,128)}) %all-reduce.15.cloned.1.call-update) | async-done | bytes 262160 | tf_op jit(solution)/shard_map/psum | solution.py:54
  326.3 11.7 cholesky.221
  348.5 11.7 cholesky.238
  364.0 12.1 %cholesky.253 = f32[128,128]{1,0:T(8,128)S(1)} custom-call(f32[128,128]{1,0:T(8,128)S(1)} %fusion.69), custom_call_target="Cholesky" | custom-call | tf_op jit(solution)/shard_map/jit(cholesky)/cholesky | solution.py:24
  390.3 42.7 %conditional.8 = (f32[256,256]{1,0:T(8,128)S(1)}) conditional(s32[]{:T(128)} %convert_element_type.28, () %tuple.53, (pred[]{:T(512)}, f32[256,256]{0,1:T(8,128)S(1)}, f32[256,128]{0,1:T(8,128)S(1)}, f32[4096,256]{1,0:T(8,128)}, f32[256,256]{0,1:T(8,128)S(1)}) %tuple.167), branch_computations={%region_13.17_spmd, %region_14.19_spmd} | conditional | flops 4907548672 | bytes 23855310 | solution.py:79
  394.7 19.7 %custom-call.21 = f32[2,128,128]{1,2,0:T(8,128)S(1)} custom-call(f32[2,128,128]{2,1,0:T(8,128)S(1)} %get-tuple-element.113), custom_call_target="InvertDiagBlocksLowerTriangular" | custom-call | tf_op jit(solution)/shard_map/cond/branch_1_fun/jit(_solve_triangular)/triangular_solve | solution.py:65
  433.9 91.5 %all-reduce.17.cloned.1.call-done = f32[256,256]{0,1:T(8,128)} async-done(((f32[256,256]{0,1:T(8,128)}), f32[256,256]{0,1:T(8,128)}) %all-reduce.17.cloned.1.call-update) | async-done | bytes 262160 | tf_op jit(solution)/shard_map/psum | solution.py:80
  529.0 11.7 cholesky.264
  552.9 28.4 %all-reduce.19.cloned.1.call-done = f32[256,128]{0,1:T(8,128)} async-done(((f32[256,128]{0,1:T(8,128)}), f32[256,128]{0,1:T(8,128)}) %all-reduce.19.cloned.1.call-update) | async-done | bytes 131088 | tf_op jit(solution)/shard_map/psum | solution.py:13
  588.6 131.1 %all-reduce.21.cloned.1.call-done = f32[256,256]{0,1:T(8,128)} async-done(((f32[256,256]{0,1:T(8,128)}), f32[256,256]{0,1:T(8,128)}) %all-reduce.21.cloned.1.call-update) | async-done | bytes 262160 | tf_op jit(solution)/shard_map/psum | solution.py:80
  721.5 11.7 cholesky.275
  749.7 19.7 %custom-call.28 = f32[2,128,128]{1,2,0:T(8,128)S(1)} custom-call(f32[2,128,128]{2,1,0:T(8,128)S(1)} %get-tuple-element.115), custom_call_target="InvertDiagBlocksLowerTriangular" | custom-call | tf_op jit(solution)/shard_map/jit(_solve_triangular)/triangular_solve | solution.py:65
  786.7 95.5 %all-gather.7.cloned.1.call-done = f32[1024,2048]{1,0:T(8,128)} async-done(((f32[128,2048]{1,0:T(8,128)}), f32[1024,2048]{1,0:T(8,128)}) %all-gather.7.cloned.1.call-update) | async-done | bytes 8388624 | tf_op jit(solution)/shard_map/all_gather | solution.py:92
  883.5 129.1 %all-reduce.23.cloned.1.call-done = f32[8,128,128]{1,2,0:T(8,128)} async-done(((f32[8,128,128]{1,2,0:T(8,128)}), f32[8,128,128]{1,2,0:T(8,128)}) %all-reduce.23.cloned.1.call-update) | async-done | bytes 524304 | tf_op jit(solution)/shard_map/psum | solution.py:112
  1013.5 33.1 %all-reduce.25.cloned.1.call-done = f32[8,128,128]{1,2,0:T(8,128)} async-done(((f32[8,128,128]{1,2,0:T(8,128)}), f32[8,128,128]{1,2,0:T(8,128)}) %all-reduce.25.cloned.1.call-update) | async-done | bytes 524304 | tf_op jit(solution)/shard_map/psum | solution.py:13
  1046.6 38.8 %conditional.11 = (f32[8,128,128]{1,2,0:T(8,128)}) conditional(s32[]{:T(128)} %convert_element_type.28, () %tuple.56, (pred[]{:T(512)}, f32[8,128,128]{1,2,0:T(8,128)}, f32[8,128,128]{1,2,0:T(8,128)S(1)}, f32[8,128,2048]{2,1,0:T(8,128)}, f32[2048,128]{1,0:T(8,128)S(1)}) %tuple.172), branch_computations={%region_24.29_spmd, %region_25.30_spmd} | conditional | flops 6442582016 | bytes 46661640 | solution.py:111
  1069.2 16.2 %convolution_bitcast_fusion.1 = f32[8,128,128]{1,2,0:T(8,128)} fusion(f32[8,2048,128]{2,1,0:T(8,128)} %reshape.52, f32[2048,128]{1,0:T(8,128)S(1)} %get-tuple-element.89), kind=kOutput, calls=%fused_computation.2 | convolution fusion | flops 3221225472 | bytes 9961472 | tf_op jit(solution)/shard_map/cond/branch_1_fun/cb,qcy->qby/dot_general | solution.py:102
  1087.5 92.6 %all-reduce.27.cloned.1.call-done = f32[8,128,128]{1,2,0:T(8,128)} async-done(((f32[8,128,128]{1,2,0:T(8,128)}), f32[8,128,128]{1,2,0:T(8,128)}) %all-reduce.27.cloned.1.call-update) | async-done | bytes 524304 | tf_op jit(solution)/shard_map/psum | solution.py:112
  (179 shorter events, 193.7 us)
Async XLA Ops:
  7.2 518.2 %copy-start = (f32[256,128]{1,0:T(8,128)S(1)}, f32[256,128]{1,0:T(8,128)}, u32[]{:S(2)}) copy-start(f32[256,128]{1,0:T(8,128)} %param.22) | copy-start | bytes 393220
  7.2 128.7 %all-reduce.11.cloned.1.call-start = ((), (), s32[]{:S(2)}) async-start(), calls=%async_computation | async-start | bytes 524288 | tf_op jit(solution)/shard_map/psum | solution.py:54
  16.1 189.5 %all-reduce.13.cloned.1.call-start = ((), (), s32[]{:S(2)}) async-start(), calls=%async_computation.1 | async-start | bytes 524288 | tf_op jit(solution)/shard_map/psum | solution.py:13
  173.0 151.1 %all-reduce.15.cloned.1.call-start = ((), (), s32[]{:S(2)}) async-start(), calls=%async_computation.2 | async-start | bytes 524288 | tf_op jit(solution)/shard_map/psum | solution.py:54
  206.5 153.8 %copy-start.3 = (f32[256,256]{0,1:T(8,128)S(1)}, f32[256,256]{0,1:T(8,128)}, u32[]{:S(2)}) copy-start(f32[256,256]{0,1:T(8,128)} %all-reduce.11.cloned.1.call-done) | copy-start | bytes 786436
  206.5 153.8 %copy-start.8 = (f32[256,128]{1,0:T(8,128)S(1)}, f32[256,128]{1,0:T(8,128)}, u32[]{:S(2)}) copy-start(f32[256,128]{1,0:T(8,128)} %param.23) | copy-start | bytes 393220
  230.4 295.0 %all-reduce.17.cloned.1.call-start = ((), (), s32[]{:S(2)}) async-start(), calls=%async_computation.3 | async-start | bytes 524288 | tf_op jit(solution)/shard_map/psum | solution.py:80
  433.9 147.4 %all-reduce.19.cloned.1.call-start = ((), (), s32[]{:S(2)}) async-start(), calls=%async_computation.4 | async-start | bytes 262144 | tf_op jit(solution)/shard_map/psum | solution.py:13
  552.9 166.9 %all-reduce.21.cloned.1.call-start = ((), (), s32[]{:S(2)}) async-start(), calls=%async_computation.5 | async-start | bytes 524288 | tf_op jit(solution)/shard_map/psum | solution.py:80
  581.3 163.0 %copy-start.7 = (f32[256,128]{0,1:T(8,128)S(1)}, f32[256,128]{0,1:T(8,128)}, u32[]{:S(2)}) copy-start(f32[256,128]{0,1:T(8,128)} %fusion.24) | copy-start | bytes 393220
  588.6 195.9 %all-gather.5.cloned.1.call-start = ((), (), s32[]{:S(2)}) async-start(), calls=%async_computation.9 | async-start | bytes 1179648 | tf_op jit(solution)/shard_map/all_gather | solution.py:93
  745.4 136.8 %all-gather.7.cloned.1.call-start = ((), (), s32[]{:S(2)}) async-start(), calls=%async_computation.10 | async-start | bytes 9437184 | tf_op jit(solution)/shard_map/all_gather | solution.py:92
  776.9 3.6 copy-start.4
  783.0 229.6 %all-reduce.23.cloned.1.call-start = ((), (), s32[]{:S(2)}) async-start(), calls=%async_computation.6 | async-start | bytes 1048576 | tf_op jit(solution)/shard_map/psum | solution.py:112
  882.6 0.8 copy-start.5
  883.4 163.2 %all-reduce.25.cloned.1.call-start = ((), (), s32[]{:S(2)}) async-start(), calls=%async_computation.7 | async-start | bytes 1048576 | tf_op jit(solution)/shard_map/psum | solution.py:13
  1013.5 166.6 %all-reduce.27.cloned.1.call-start = ((), (), s32[]{:S(2)}) async-start(), calls=%async_computation.8 | async-start | bytes 1048576 | tf_op jit(solution)/shard_map/psum | solution.py:112
  1046.6 39.6 %copy-start.2 = (f32[128,2048]{1,0:T(8,128)S(1)}, f32[128,2048]{1,0:T(8,128)}, u32[]{:S(2)}) copy-start(f32[128,2048]{1,0:T(8,128)} %fusion.107) | copy-start | bytes 3145732
  1085.4 94.7 %copy-start.6 = (f32[8,128,128]{1,2,0:T(8,128)S(1)}, f32[8,128,128]{1,2,0:T(8,128)}, u32[]{:S(2)}) copy-start(f32[8,128,128]{1,2,0:T(8,128)} %all-reduce.23.cloned.1.call-done) | copy-start | bytes 1572868
  1085.4 96.8 %copy-start.1 = (f32[256,128]{1,0:T(8,128)S(1)}, f32[256,128]{1,0:T(8,128)}, u32[]{:S(2)}) copy-start(f32[256,128]{1,0:T(8,128)} %param.22) | copy-start | bytes 393220
Sparse Core Ops, SparseCore 0:
  16.2 119.6 all-reduce.10
  173.1 32.3 all-reduce.12
  230.5 93.5 all-reduce.14
  434.0 91.3 all-reduce.16
  553.0 28.2 all-reduce.18
  588.7 131.0 all-reduce.20
  745.5 37.0 all-gather.4
  785.1 96.9 all-gather.6
  886.3 126.2 all-reduce.22
  1015.6 30.9 all-reduce.24
  1085.6 94.4 all-reduce.26
where the time goes:
time: 1200 us; the launch traced here: 1190 us
  waiting for transfers between devices  835 us (70%)
  other arithmetic  183 us (15%)
  matrix products  84.3 us (7%)
  local copies, waits for them, and re-layouts  48.8 us (4%)
  between operations  17.2 us (1%)
  starting transfers between devices  12.7 us (1%)
    psum x4, waiting for transfers between devices, local(): summed = jnp.where(active, lax.psum(partial_value, 'row'), identity)  424 us
    psum x2, waiting for transfers between devices, local(): summed = lax.psum(partial_value, 'row')  222 us
    all_gather x1, waiting for transfers between devices, local(): lax.all_gather(shaped[None], 'vec', axis=0, tiled=True)  95.5 us
    psum x3, waiting for transfers between devices, broadcast(): return lax.psum(block, axis)  94 us
    another operation x13, other arithmetic, local(): factor = jnp.linalg.cholesky(summed)  68.5 us
    dot_general x17, matrix products, product(): jnp.dot(left_mat, right_mat, precision=lax.Precision.HIGHEST, preferred_e...  49.5 us
    another operation x8, other arithmetic, right_map_of(): jax.scipy.linalg.solve_triangular(lower_own, incoming_frame, lower=True,...  39.4 us
    another operation x9, other arithmetic, orthonormal(): chol_low = jnp.linalg.cholesky(product(powered.T, powered))  37.6 us
  transfers between devices with their start and end apart: 11, of which 10 were waited for; matrix products, arithmetic and copies ran while one was open for 4% of the time, Pallas kernels for 0%

commit v1 on v0

v1 whole, which is shorter than its diff:
```python
import functools
import math

import jax
import jax.numpy as jnp
from jax import lax
from jax.experimental import pallas as pl
from jax.experimental.pallas import tpu as pltpu
from jax.sharding import PartitionSpec as P

MESH = pl.DeviceIdType.MESH
F32 = jnp.float32
BF16 = jnp.bfloat16
HIGHEST = lax.Precision.HIGHEST
PANEL = 16


def dot(a, b):
    return jnp.dot(a, b, preferred_element_type=F32)


def dot_nt(a, b):
    return lax.dot_general(a, b, (((1,), (1,)), ((), ())), preferred_element_type=F32)


def dot_tn(a, b):
    return lax.dot_general(a, b, (((0,), (0,)), ((), ())), preferred_element_type=F32)


def fdot(a, b):
    return jnp.dot(a, b, precision=HIGHEST, preferred_element_type=F32)


def fdot_nt(a, b):
    return lax.dot_general(
        a, b, (((1,), (1,)), ((), ())), precision=HIGHEST, preferred_element_type=F32
    )


def fdot_tn(a, b):
    return lax.dot_general(
        a, b, (((0,), (0,)), ((), ())), precision=HIGHEST, preferred_element_type=F32
    )


def split(x):
    hi = x.astype(BF16)
    lo = (x - hi.astype(F32)).astype(BF16)
    return hi, lo


def eliminate(xs, n, nb):
    lane = lax.broadcasted_iota(jnp.int32, (nb, n), 1)
    sub = lax.broadcasted_iota(jnp.int32, (nb, n), 0)

    def panel(t, carry):
        j0 = pl.multiple_of(t * nb, nb)
        v = xs[pl.ds(j0, nb), :]
        rolled = pltpu.roll(v, lax.rem(n - j0, n), 1)
        cols = [jnp.broadcast_to(rolled[:, k : k + 1], (nb, n)) for k in range(nb)]
        inv = jnp.zeros((nb, n), F32)
        for k in range(nb):
            rp = 1.0 / jnp.broadcast_to(cols[k][k : k + 1, :], (nb, n))
            inv = jnp.where(sub == k, rp, inv)
            f = jnp.where(sub > k, cols[k] * rp, 0.0)
            for m in range(k + 1, nb):
                cols[m] = cols[m] - f * cols[m][k : k + 1, :]
            pivot_row = v[k : k + 1, :]
            pivot_row = jnp.where(lane[:1] == j0 + k, 2.0 * pivot_row, pivot_row)
            v = v - f * pivot_row
        below = jnp.where(lane >= j0 + nb, v, 0.0)
        scaled = jnp.where(lane == j0 + sub, 2.0 * v, v) * inv
        xs[...] = xs[...] - fdot_tn(below, scaled)
        xs[pl.ds(j0, nb), :] = v
        return carry

    lax.fori_loop(0, n // nb, panel, 0)


def factors(xs, n):
    x = xs[...]
    rows = lax.broadcasted_iota(jnp.int32, (n, n), 0)
    lanes = lax.broadcasted_iota(jnp.int32, (n, n), 1)
    diag = jnp.where(rows == lanes, x, 0.0)
    by_row = 1.0 / jnp.sqrt(jnp.sum(diag, axis=1, keepdims=True))
    by_lane = 1.0 / jnp.sum(diag, axis=0, keepdims=True)
    lower = jnp.where(rows > lanes, x * by_lane, jnp.where(rows == lanes, 1.0, 0.0))
    upper = jnp.where(rows <= lanes, x, 0.0)
    return lower * by_row, upper * by_row


def kernel(
    sizes,
    g_hbm, w_ref, xw_ref,
    rounded_ref, bases_ref, margins_ref,
    stage, ghi, glo, gthi, gtlo, part, rs, full, lower_ref, zt_ref, xs, xcat, nw,
    ring, epart, ers, ered, xrecv, efull, ein,
    load_sem, rs_send, rs_recv, ag_send, ag_recv, pair_send, pair_recv,
    ring_send, ring_recv, ers_send, ers_recv, x_send, x_recv, eag_send, eag_recv,
):
    rank, kept, modes, rows_n, vecs = sizes
    half = vecs // 2
    mh = modes // 2
    ch = rank // rows_n
    ech = kept // rows_n
    blocks = vecs + 2 * (half - 1)
    core = lax.axis_index("cores")
    row = lax.axis_index("row")
    vec = lax.axis_index("vec")
    other = 1 - core

    pieces = load_sem.shape[0]
    prow = rank * modes // pieces
    loads = [
        pltpu.make_async_copy(
            g_hbm.at[pl.ds(t * prow, prow), pl.ds(h * 128, 128)],
            stage.at[h, pl.ds(t * prow, prow)],
            load_sem.at[t, h],
        )
        for t in range(pieces)
        for h in range(rank // 128)
    ]
    for load in loads:
        load.start()

    barrier = pltpu.get_barrier_semaphore()

    def greet(d, carry):
        there = lax.rem(row + d, rows_n)
        pl.semaphore_signal(barrier, inc=1, device_id=(core, there, vec), device_id_type=MESH)
        pl.semaphore_signal(barrier, inc=1, device_id=(other, there, vec), device_id_type=MESH)
        return carry

    lax.fori_loop(1, rows_n, greet, 0)
    pl.semaphore_signal(barrier, inc=1, device_id=(other, row, vec), device_id_type=MESH)
    away = sorted({d % vecs for d in range(-(half - 1), half)} | {1, vecs - 1})
    away = [d for d in away if d != 0]
    for d in away:
        pl.semaphore_signal(
            barrier, inc=1, device_id=(core, row, lax.rem(vec + d, vecs)), device_id_type=MESH
        )

    def meet():
        pl.semaphore_wait(barrier, 2 * (rows_n - 1) + 1 + len(away))

    def remote(src, dst, send, recv, to):
        return pltpu.make_async_remote_copy(
            src_ref=src, dst_ref=dst, send_sem=send, recv_sem=recv,
            device_id=to, device_id_type=MESH,
        )

    def pair_copy(src, dst, which):
        return remote(src, dst, pair_send.at[which], pair_recv.at[which], (other, row, vec))

    def scatter(which, to_core, first):
        def send(d, carry):
            there = lax.rem(row + d, rows_n)
            remote(
                part.at[pl.ds(there * ch, ch)], rs.at[which, d],
                rs_send.at[which], rs_recv.at[which], (to_core, there, vec),
            ).start()
            return carry

        lax.fori_loop(first, rows_n, send, 0)

    def scatter_sent(which, first):
        count = (rows_n - first) * ch
        remote(
            part.at[pl.ds(0, count)], part.at[pl.ds(0, count)],
            rs_send.at[which], rs_recv.at[which], (other, row, vec),
        ).wait_send()

    def scatter_arrived(which, first):
        view = rs.at[which, pl.ds(first, rows_n - first)]
        remote(
            view, view, rs_send.at[which], rs_recv.at[which], (other, row, vec)
        ).wait_recv()

    def gather(which):
        mine = full.at[which, pl.ds(row * ch, ch)]

        def send(d, carry):
            there = lax.rem(row + d, rows_n)
            remote(
                mine, mine, ag_send.at[which], ag_recv.at[which], (core, there, vec)
            ).start()
            return carry

        lax.fori_loop(1, rows_n, send, 0)
        view = full.at[which, pl.ds(0, (rows_n - 1) * ch)]
        done = remote(view, view, ag_send.at[which], ag_recv.at[which], (other, row, vec))
        done.wait_recv()
        done.wait_send()

    def sum_rows(which):
        scatter(which, core, 1)
        scatter_arrived(which, 1)
        total = part[pl.ds(row * ch, ch), :]
        for d in range(1, rows_n):
            total = total + rs[which, d]
        full[which, pl.ds(row * ch, ch), :] = total
        scatter_sent(which, 1)
        gather(which)

    def by_mode(with_transposes):
        def body(i, carry):
            x = jnp.concatenate(
                [stage[h, pl.ds(i, rank, stride=modes), :] for h in range(rank // 128)], axis=1
            )
            hi, lo = split(x)
            ghi[i] = hi
            glo[i] = lo
            if with_transposes:
                hi, lo = split(x.T)
                gthi[i] = hi
                gtlo[i] = lo
            return carry

        lax.fori_loop(0, modes, body, 0)

    def left_gram(z):
        zhi, zlo = split(z)
        part[...] = jnp.zeros_like(part)

        def body(i, carry):
            x = dot(ghi[i], zhi) + dot(ghi[i], zlo) + dot(glo[i], zhi)
            hi, lo = split(x)
            both = jnp.concatenate([hi, lo], axis=1)
            swapped = jnp.concatenate([lo, hi], axis=1)
            xcat[i] = both
            part[...] += dot_nt(both, both) + dot_nt(both, swapped)
            return carry

        lax.fori_loop(0, modes, body, 0)

    def whiten(yt):
        xs[...] = fdot_nt(yt, yt)
        eliminate(xs, kept, PANEL)
        return factors(xs, kept)[0]

    def shape_cores(ft):
        fhi, flo = split(ft)
        scale = math.sqrt(kept * modes * rows_n)

        def body(i, carry):
            both = xcat[i]
            r = dot(fhi, both)
            n = r[:, :kept] + r[:, kept:] + dot(flo, both[:, :kept])
            rounded_ref[pl.ds(i, kept, stride=modes), :] = n * scale
            hi, lo = split(n)
            line = jnp.concatenate([hi, lo], axis=1)
            nw[i] = jnp.concatenate([line, line], axis=0)
            at = pl.multiple_of(lax.rem(i, mh) * kept, kept)
            ring[i // mh, 0, pl.ds(at, kept), :] = n.T
            return carry

        lax.fori_loop(0, modes, body, 0)

    def ring_copy(side, k, count):
        to = lax.rem(vec + (1 if side == 0 else vecs - 1), vecs)
        return remote(
            ring.at[side, k, pl.ds(0, count)], ring.at[side, k + 1, pl.ds(0, count)],
            ring_send.at[side, k], ring_recv.at[side, k], (core, row, to),
        )

    def round_ring(count, work):
        for k in range(half):
            for side in (0, 1):
                if k > 0:
                    ring_copy(side, k - 1, count).wait_recv()
                ring_copy(side, k, count).start()
            work(k)
        for side in (0, 1):
            ring_copy(side, half - 1, count).wait_recv()
        work(half)
        for k in range(half):
            for side in (0, 1):
                ring_copy(side, k, count).wait_send()

    def carry_modes(side, k, et):
        hi, lo = split(et)
        line = jnp.concatenate([hi, lo], axis=1)
        weights = jnp.concatenate([line, line], axis=0)

        def body(i, acc):
            at = pl.multiple_of(i * kept, kept)
            hi, lo = split(ring[side, k, pl.ds(at, kept), :])
            r = dot(jnp.concatenate([hi, lo], axis=1), weights)
            hi, lo = split(r[:, :kept] + r[:, kept:])
            return acc + dot(jnp.concatenate([hi, lo], axis=1), nw[side * mh + i])

        acc = lax.fori_loop(0, mh, body, jnp.zeros((kept, 2 * kept), F32))
        return acc[:, :kept] + acc[:, kept:]

    def margin_work(k, env):
        down = lax.rem(vec + vecs - k, vecs)
        up = lax.rem(vec + k, vecs)
        first = carry_modes(0, k, env(0, k, down))
        second = carry_modes(1, k, env(1, k, up))
        if k == 0 or k == half:
            epart[down] = first + second
        else:
            epart[down] = first
            epart[up] = second
            epart[vecs + k - 1] = first.T
            epart[vecs + half - 1 + k - 1] = second.T

    def sum_margins():
        def send(d, carry):
            there = lax.rem(row + d, rows_n)
            remote(
                epart.at[:, pl.ds(there * ech, ech), :], ers.at[d],
                ers_send, ers_recv, (core, there, vec),
            ).start()
            return carry

        lax.fori_loop(1, rows_n, send, 0)
        view = ers.at[pl.ds(1, rows_n - 1)]
        done = remote(view, view, ers_send, ers_recv, (other, row, vec))
        done.wait_recv()
        total = epart[:, pl.ds(row * ech, ech), :]
        for d in range(1, rows_n):
            total = total + ers[d]
        ered[...] = total
        done.wait_send()
        count = half - 1
        for d in range(1, half):
            remote(
                ered.at[vecs + d - 1], xrecv.at[d - 1], x_send, x_recv,
                (core, row, lax.rem(vec + vecs - d, vecs)),
            ).start()
            remote(
                ered.at[vecs + count + d - 1], xrecv.at[count + d - 1], x_send, x_recv,
                (core, row, lax.rem(vec + d, vecs)),
            ).start()
        done = remote(xrecv, xrecv, x_send, x_recv, (other, row, vec))
        done.wait_recv()
        done.wait_send()
        for d in range(1, half):
            up = lax.rem(vec + d, vecs)
            down = lax.rem(vec + vecs - d, vecs)
            ered[up] = ered[up] + xrecv[d - 1]
            ered[down] = ered[down] + xrecv[count + d - 1]
        mine = efull.at[:, pl.ds(row * ech, ech), :]
        efull[:, pl.ds(row * ech, ech), :] = ered[pl.ds(0, vecs)]

        def spread(d, carry):
            there = lax.rem(row + d, rows_n)
            remote(mine, mine, eag_send, eag_recv, (core, there, vec)).start()
            return carry

        lax.fori_loop(1, rows_n, spread, 0)
        view = efull.at[:, pl.ds(0, (rows_n - 1) * ech), :]
        done = remote(view, view, eag_send, eag_recv, (other, row, vec))
        done.wait_recv()
        done.wait_send()

    def margins_out():
        for q in range(vecs):
            margins_ref[:, q * kept : (q + 1) * kept] = efull[q].T

    bases_scale = math.sqrt(rank)

    @pl.when(core == 0)
    def front():
        part[...] = jnp.zeros_like(part)
        full[0] = jnp.zeros_like(part)
        for t in range(pieces):
            for h in range(rank // 128):
                loads[t * (rank // 128) + h].wait()
            hi, lo = split(
                jnp.concatenate(
                    [stage[h, pl.ds(t * prow, prow), :] for h in range(rank // 128)], axis=1
                )
            )
            part[...] += dot_tn(hi, hi)
            full[2] = dot_tn(hi, lo) if t == 0 else full[2] + dot_tn(hi, lo)
        cross = full[2]
        part[...] += cross + cross.T
        meet()
        scatter(0, other, 0)
        by_mode(False)
        wt = w_ref[...].T
        scatter_sent(0, 0)

        pair_copy(full.at[0], full.at[0], 0).wait_recv()
        xs[...] = full[0, :kept, :kept]
        eliminate(xs, kept, PANEL)
        kinv, kt = factors(xs, kept)
        lower_ref[:kept, :kept] = kt.T
        lower_ref[:kept, kept:] = jnp.zeros((kept, rank - kept), F32)
        left = fdot_nt(full[0, kept:, :kept], kinv)
        lower_ref[kept:, :kept] = left
        xs[...] = full[0, kept:, kept:] - fdot_nt(left, left)
        eliminate(xs, kept, PANEL)
        kinv, kt = factors(xs, kept)
        lower_ref[kept:, kept:] = kt.T
        to_pair = pair_copy(lower_ref, lower_ref, 1)
        to_pair.start()

        pair_copy(zt_ref, zt_ref, 2).wait_recv()
        left_gram(zt_ref[...].T)
        sum_rows(1)
        gram = full[1]
        yt = fdot(fdot(wt, gram), gram)
        ut = fdot(whiten(yt), yt)
        bases_ref[...] = ut.T * bases_scale
        shape_cores(ut)
        for side in (0, 1):
            ring[side, 0, pl.ds(mh * kept, kept), :] = ut[:, :kept]
            ring[side, 0, pl.ds((mh + 1) * kept, kept), :] = ut[:, kept:]

        def env(side, k, q):
            a = ring[side, k, pl.ds(mh * kept, kept), :]
            b = ring[side, k, pl.ds((mh + 1) * kept, kept), :]
            c = ring[0, 0, pl.ds(mh * kept, kept), :]
            d = ring[0, 0, pl.ds((mh + 1) * kept, kept), :]
            return fdot_nt(a, c) + fdot_nt(b, d)

        round_ring((mh + 2) * kept, lambda k: margin_work(k, env))
        sum_margins()
        onward = pair_copy(efull, ein, 3)
        onward.start()
        margins_out()
        onward.wait_send()
        to_pair.wait_send()

    @pl.when(core == 1)
    def back():
        for load in loads:
            load.wait()
        by_mode(True)
        wt = w_ref[...].T
        xwt = xw_ref[...].T
        meet()
        scatter_arrived(0, 0)
        total = rs[0, 0]
        for d in range(1, rows_n):
            total = total + rs[0, d]
        full[0, pl.ds(row * ch, ch), :] = total
        gather(0)
        to_pair = pair_copy(full.at[0], full.at[0], 0)
        to_pair.start()

        chi, clo = split(full[0])
        part[...] = jnp.zeros_like(part)

        def body(i, carry):
            h = dot(gthi[i], chi) + dot(gthi[i], clo) + dot(gtlo[i], chi)
            hi, lo = split(h)
            part[...] += dot(hi, ghi[i]) + dot(hi, glo[i]) + dot(lo, ghi[i])
            return carry

        lax.fori_loop(0, modes, body, 0)
        sum_rows(1)
        gram = full[1]
        yt = fdot(fdot(xwt, gram), gram)
        ut = fdot(whiten(yt), yt)
        left_gram(ut.T)
        sum_rows(2)

        pair_copy(lower_ref, lower_ref, 1).wait_recv()
        low = lower_ref[...]
        vt = fdot_nt(wt, low)
        pt = fdot(fdot(fdot(vt, full[2]), full[0]), full[2])
        yt = fdot(pt, low)
        kinv = whiten(yt)
        zt_ref[...] = fdot(kinv, pt)
        z_pair = pair_copy(zt_ref, zt_ref, 2)
        z_pair.start()
        ut = fdot(kinv, yt)
        bases_ref[...] = ut.T * bases_scale
        shape_cores(fdot_nt(ut, low))
        round_ring(mh * kept, lambda k: None)
        pair_copy(efull, ein, 3).wait_recv()
        for k in range(half + 1):
            margin_work(k, lambda side, k, q: ein[q])
        sum_margins()
        margins_out()
        to_pair.wait_send()
        z_pair.wait_send()


def build(mesh):
    rows_n = mesh.shape["row"]
    vecs = mesh.shape["vec"]

    def local(train_cores, sketch, exit_sketch):
        _, rank, modes, _ = train_cores.shape
        kept = sketch.shape[1]
        half = vecs // 2
        mh = modes // 2
        ch = rank // rows_n
        ech = kept // rows_n
        blocks = vecs + 2 * (half - 1)
        dma = pltpu.SemaphoreType.DMA
        vmem = pl.BlockSpec(memory_space=pltpu.VMEM)
        rounded, bases, margins = pl.pallas_call(
            functools.partial(kernel, (rank, kept, modes, rows_n, vecs)),
            out_shape=(
                jax.ShapeDtypeStruct((kept * modes, kept), F32),
                jax.ShapeDtypeStruct((rank, kept), F32),
                jax.ShapeDtypeStruct((kept, vecs * kept), F32),
            ),
            in_specs=[pl.BlockSpec(memory_space=pl.ANY), vmem, vmem],
            out_specs=(vmem, vmem, vmem),
            scratch_shapes=[
                pltpu.VMEM((rank // 128, rank * modes, 128), F32),
                pltpu.VMEM((modes, rank, rank), BF16),
                pltpu.VMEM((modes, rank, rank), BF16),
                pltpu.VMEM((modes, rank, rank), BF16),
                pltpu.VMEM((modes, rank, rank), BF16),
                pltpu.VMEM((rank, rank), F32),
                pltpu.VMEM((3, rows_n, ch, rank), F32),
                pltpu.VMEM((3, rank, rank), F32),
                pltpu.VMEM((rank, rank), F32),
                pltpu.VMEM((kept, rank), F32),
                pltpu.VMEM((kept, kept), F32),
                pltpu.VMEM((modes, rank, 2 * kept), BF16),
                pltpu.VMEM((modes, 2 * kept, 2 * kept), BF16),
                pltpu.VMEM((2, half + 1, (mh + 2) * kept, kept), F32),
                pltpu.VMEM((blocks, kept, kept), F32),
                pltpu.VMEM((rows_n, blocks, ech, kept), F32),
                pltpu.VMEM((blocks, ech, kept), F32),
                pltpu.VMEM((2 * (half - 1), ech, kept), F32),
                pltpu.VMEM((vecs, kept, kept), F32),
                pltpu.VMEM((vecs, kept, kept), F32),
                dma((8, rank // 128)),
                dma((3,)), dma((3,)), dma((3,)), dma((3,)),
                dma((4,)), dma((4,)),
                dma((2, half)), dma((2, half)),
                dma, dma, dma, dma, dma, dma,
            ],
            compiler_params=pltpu.CompilerParams(
                collective_id=0, has_side_effects=True, vmem_limit_bytes=58 * 1024 * 1024
            ),
        )(train_cores.reshape(rank * modes, rank), sketch, exit_sketch)
        return (
            rounded.reshape(1, kept, modes, kept),
            bases[None],
            margins[None],
        )

    return local


def solution(mesh):
    return jax.shard_map(
        build(mesh),
        mesh=mesh,
        in_specs=(P("vec", "cores", "row", None), P("cores", None), P()),
        out_specs=(
            P("vec", "cores", "row", None),
            P("vec", "cores", None),
            P("vec", "cores", None),
        ),
        check_vma=False,
    )
```

time: 1200 us -> 222 us (0.18)
  waiting for transfers between devices: 835 us -> 0 us
  Pallas kernels: 0 us -> 215 us
  other arithmetic: 183 us -> 0 us
  matrix products: 84.3 us -> 0 us
  local copies, waits for them, and re-layouts: 48.8 us -> 5.71 us
  between operations: 17.2 us -> 0.64 us
  starting transfers between devices: 12.7 us -> 0 us
    psum x9 -> x0, waiting for transfers between devices: 740 us -> none  [the longest x4 424 us: local(): summed = jnp.where(active, lax.psum(partial_value, 'row'), identity)]
    pallas_call x0 -> x1, Pallas kernels: none -> 215 us  [local(): pl.pallas_call(functools.partial(kernel, (rank, kept, modes, rows_n, vecs...]
    another operation x36 -> x0, other arithmetic: 177 us -> none  [the longest x13 68.5 us: local(): factor = jnp.linalg.cholesky(summed)]
    all_gather x2 -> x0, waiting for transfers between devices: 95.5 us -> none  [the longest x1 95.5 us: local(): lax.all_gather(shaped[None], 'vec', axis=0, tiled=True)]
    dot_general x20 -> x0, matrix products: 79.6 us -> none  [the longest x17 49.5 us: product(): jnp.dot(left_mat, right_mat, precision=lax.Precision.HIGHEST, preferred_e...]
    reshape x5 -> x0, local copies, waits for them, and re-layouts: 19.2 us -> none  [the longest x1 9.28 us: margin_terms(): carried = carried.reshape(vector_count, kept_rank * mode_count, kept_rank)]
    psum x9 -> x0, starting transfers between devices: 12.4 us -> none  [the longest x3 11.9 us: broadcast(): return lax.psum(block, axis)]
  transfers between devices with their start and end apart: 11 -> 0, of which waited for: 10 -> 0; matrix products, arithmetic and copies ran while one was open for 4% -> 0% of each run, Pallas kernels for 0% -> 0%
where the time goes in v1:
time: 222 us
  Pallas kernels  215 us (97%)
  local copies, waits for them, and re-layouts  5.71 us (3%)
    pallas_call x1, Pallas kernels, local(): pl.pallas_call(functools.partial(kernel, (rank, kept, modes, rows_n, vecs...  215 us
    unnamed x3, local copies, waits for them, and re-layouts  5.71 us

profile of v1, /device:TPU:1, one launch (start us, length us, event | category | flops | bytes accessed | tf_op | source)
XLA Modules:
  0.0 221.8 jit_solution(3525853016175063372)
XLA Ops:
  0.6 215.5 %shard_map.58 = (f32[2048,128]{1,0:T(8,128)}, f32[256,128]{1,0:T(8,128)}, f32[128,1024]{1,0:T(8,128)}) custom-call(f32[4096,256]{1,0:T(8,128)} %bitcast.4, f32[256,128]{1,0:T(8,128)} %w_ref.1, f32[256,128]{1,0:T(8,128)} %xw_ref.1), custom_call_target="tpu_custom_call" | custom-call | tf_op jit(solution)/shard_map/pallas_call | solution.py:498
  216.1 2.3 %copy.9 = f32[1,128,16,128]{3,2,1,0:T(8,128)} copy(f32[1,128,16,128]{3,2,1,0:T(8,128)} %bitcast.5) | data formatting | bytes 2097152
  218.4 1.6 copy.10
  219.9 1.9 copy.11

commit v2 on v1

--- a/solution.py
+++ b/solution.py
@@ -13,6 +13,7 @@
 BF16 = jnp.bfloat16
 HIGHEST = lax.Precision.HIGHEST
 PANEL = 16
+GROUP = 4
 
 
 def dot(a, b):
@@ -47,6 +48,11 @@
     hi = x.astype(BF16)
     lo = (x - hi.astype(F32)).astype(BF16)
     return hi, lo
+
+
+def beside(x, count):
+    n = x.shape[0] // count
+    return jnp.concatenate([x[m * n : (m + 1) * n] for m in range(count)], axis=1)
 
 
 def eliminate(xs, n, nb):
@@ -94,16 +100,15 @@
     g_hbm, w_ref, xw_ref,
     rounded_ref, bases_ref, margins_ref,
     stage, ghi, glo, gthi, gtlo, part, rs, full, lower_ref, zt_ref, xs, xcat, nw,
-    ring, epart, ers, ered, xrecv, efull, ein,
+    ring, epart, ers, xsend, xrecv, efull, ein, rounded_buf, bases_buf, margins_buf,
     load_sem, rs_send, rs_recv, ag_send, ag_recv, pair_send, pair_recv,
-    ring_send, ring_recv, ers_send, ers_recv, x_send, x_recv, eag_send, eag_recv,
+    ring_send, ring_recv, ers_send, ers_recv, x_send, x_recv, eag_send, eag_recv, out_sem,
 ):
     rank, kept, modes, rows_n, vecs = sizes
     half = vecs // 2
     mh = modes // 2
     ch = rank // rows_n
     ech = kept // rows_n
-    blocks = vecs + 2 * (half - 1)
     core = lax.axis_index("cores")
     row = lax.axis_index("row")
     vec = lax.axis_index("vec")
@@ -207,54 +212,61 @@
             x = jnp.concatenate(
                 [stage[h, pl.ds(i, rank, stride=modes), :] for h in range(rank // 128)], axis=1
             )
-            hi, lo = split(x)
-            ghi[i] = hi
-            glo[i] = lo
+            at = pl.ds(pl.multiple_of(i * rank, rank), rank)
+            ghi[at, :], glo[at, :] = split(x)
             if with_transposes:
-                hi, lo = split(x.T)
-                gthi[i] = hi
-                gtlo[i] = lo
+                gthi[at, :], gtlo[at, :] = split(x.T)
             return carry
 
         lax.fori_loop(0, modes, body, 0)
 
     def left_gram(z):
         zhi, zlo = split(z)
+        zboth = jnp.concatenate([zhi, zlo], axis=1)
         part[...] = jnp.zeros_like(part)
 
         def body(i, carry):
-            x = dot(ghi[i], zhi) + dot(ghi[i], zlo) + dot(glo[i], zhi)
+            at = pl.ds(pl.multiple_of(i * GROUP * rank, GROUP * rank), GROUP * rank)
+            r = dot(ghi[at, :], zboth)
+            x = r[:, :kept] + r[:, kept:] + dot(glo[at, :], zhi)
             hi, lo = split(x)
             both = jnp.concatenate([hi, lo], axis=1)
+            xcat[at, :] = both
             swapped = jnp.concatenate([lo, hi], axis=1)
-            xcat[i] = both
-            part[...] += dot_nt(both, both) + dot_nt(both, swapped)
-            return carry
-
-        lax.fori_loop(0, modes, body, 0)
+            wide = beside(both, GROUP)
+            part[...] += dot_nt(wide, wide) + dot_nt(wide, beside(swapped, GROUP))
+            return carry
+
+        lax.fori_loop(0, modes // GROUP, body, 0)
 
     def whiten(yt):
         xs[...] = fdot_nt(yt, yt)
         eliminate(xs, kept, PANEL)
         return factors(xs, kept)[0]
 
-    def shape_cores(ft):
+    scale = math.sqrt(kept * modes * rows_n)
+
+    def shape_cores(ft, side):
         fhi, flo = split(ft)
-        scale = math.sqrt(kept * modes * rows_n)
-
-        def body(i, carry):
-            both = xcat[i]
-            r = dot(fhi, both)
-            n = r[:, :kept] + r[:, kept:] + dot(flo, both[:, :kept])
-            rounded_ref[pl.ds(i, kept, stride=modes), :] = n * scale
-            hi, lo = split(n)
-            line = jnp.concatenate([hi, lo], axis=1)
-            nw[i] = jnp.concatenate([line, line], axis=0)
-            at = pl.multiple_of(lax.rem(i, mh) * kept, kept)
-            ring[i // mh, 0, pl.ds(at, kept), :] = n.T
-            return carry
-
-        lax.fori_loop(0, modes, body, 0)
+        group = min(GROUP, mh)
+
+        def body(t, carry):
+            for m in range(group):
+                i = side * mh + t * group + m
+                both = xcat[pl.ds(pl.multiple_of(i * rank, rank), rank), :]
+                r = dot(fhi, both)
+                n = r[:, :kept] + r[:, kept:] + dot(flo, both[:, :kept])
+                rounded_buf[pl.ds(i, kept, stride=modes), :] = n * scale
+                hi, lo = split(n)
+                line = jnp.concatenate([hi, lo], axis=1)
+                at = pl.multiple_of(i * 2 * kept, 2 * kept)
+                nw[pl.ds(at, kept), :] = line
+                nw[pl.ds(pl.multiple_of(at + kept, kept), kept), :] = line
+                at = pl.multiple_of((t * group + m) * kept, kept)
+                ring[side, 0, pl.ds(at, kept), :] = n.T
+            return carry
+
+        lax.fori_loop(0, mh // group, body, 0)
 
     def ring_copy(side, k, count):
         to = lax.rem(vec + (1 if side == 0 else vecs - 1), vecs)
@@ -263,16 +275,14 @@
             ring_send.at[side, k], ring_recv.at[side, k], (core, row, to),
         )
 
-    def round_ring(count, work):
-        for k in range(half):
-            for side in (0, 1):
-                if k > 0:
-                    ring_copy(side, k - 1, count).wait_recv()
+    def ring_step(k, count):
+        for side in (0, 1):
+            if k > 0:
+                ring_copy(side, k - 1, count).wait_recv()
+            if k < half:
                 ring_copy(side, k, count).start()
-            work(k)
-        for side in (0, 1):
-            ring_copy(side, half - 1, count).wait_recv()
-        work(half)
+
+    def ring_sent(count):
         for k in range(half):
             for side in (0, 1):
                 ring_copy(side, k, count).wait_send()
@@ -281,83 +291,113 @@
         hi, lo = split(et)
         line = jnp.concatenate([hi, lo], axis=1)
         weights = jnp.concatenate([line, line], axis=0)
-
-        def body(i, acc):
-            at = pl.multiple_of(i * kept, kept)
-            hi, lo = split(ring[side, k, pl.ds(at, kept), :])
-            r = dot(jnp.concatenate([hi, lo], axis=1), weights)
-            hi, lo = split(r[:, :kept] + r[:, kept:])
-            return acc + dot(jnp.concatenate([hi, lo], axis=1), nw[side * mh + i])
-
-        acc = lax.fori_loop(0, mh, body, jnp.zeros((kept, 2 * kept), F32))
+        hi, lo = split(ring[side, k, pl.ds(0, mh * kept), :])
+        r = dot(jnp.concatenate([hi, lo], axis=1), weights)
+        hi, lo = split(r[:, :kept] + r[:, kept:])
+        wide = beside(jnp.concatenate([hi, lo], axis=1), mh)
+        at = side * mh * 2 * kept
+        acc = dot(wide, nw[pl.ds(at, mh * 2 * kept), :])
         return acc[:, :kept] + acc[:, kept:]
 
+    def up_at(k):
+        return vecs - 1 if k == half else k
+
+    def down_at(k):
+        return 0 if k == 0 else vecs - 1 if k == half else half - 1 + k
+
+    def swap_copy(k, side):
+        to = lax.rem(vec + (vecs - k if side == 0 else k), vecs)
+        return remote(
+            xsend.at[k - 1, side], xrecv.at[k - 1, side], x_send.at[k - 1], x_recv.at[k - 1],
+            (core, row, to),
+        )
+
     def margin_work(k, env):
-        down = lax.rem(vec + vecs - k, vecs)
-        up = lax.rem(vec + k, vecs)
-        first = carry_modes(0, k, env(0, k, down))
-        second = carry_modes(1, k, env(1, k, up))
+        first = carry_modes(0, k, env(0, k))
+        second = carry_modes(1, k, env(1, k))
         if k == 0 or k == half:
-            epart[down] = first + second
+            epart[up_at(k)] = first + second
         else:
-            epart[down] = first
-            epart[up] = second
-            epart[vecs + k - 1] = first.T
-            epart[vecs + half - 1 + k - 1] = second.T
-
-    def sum_margins():
+            epart[down_at(k)] = first
+            epart[up_at(k)] = second
+            xsend[k - 1, 0] = first.T
+            xsend[k - 1, 1] = second.T
+            for side in (0, 1):
+                swap_copy(k, side).start()
+
+    def swap_done():
+        for k in range(1, half):
+            view = xrecv.at[k - 1]
+            done = remote(view, view, x_send.at[k - 1], x_recv.at[k - 1], (other, row, vec))
+            done.wait_recv()
+            done.wait_send()
+            epart[up_at(k)] += xrecv[k - 1, 0]
+            epart[down_at(k)] += xrecv[k - 1, 1]
+
+    spans = ((0, vecs - 1), (vecs - 1, 1))
+
+    def margin_scatter(g):
+        first, count = spans[g]
+
         def send(d, carry):
             there = lax.rem(row + d, rows_n)
             remote(
-                epart.at[:, pl.ds(there * ech, ech), :], ers.at[d],
-                ers_send, ers_recv, (core, there, vec),
+                epart.at[pl.ds(first, count), pl.ds(there * ech, ech), :],
+                ers.at[d, pl.ds(first, count)],
+                ers_send.at[g], ers_recv.at[g], (core, there, vec),
             ).start()
             return carry
 
         lax.fori_loop(1, rows_n, send, 0)
-        view = ers.at[pl.ds(1, rows_n - 1)]
-        done = remote(view, view, ers_send, ers_recv, (other, row, vec))
+
+    def margin_gather(g):
+        first, count = spans[g]
+        view = ers.at[pl.ds(1, rows_n - 1), pl.ds(first, count)]
+        done = remote(view, view, ers_send.at[g], ers_recv.at[g], (other, row, vec))
         done.wait_recv()
-        total = epart[:, pl.ds(row * ech, ech), :]
+        mine = pl.ds(pl.multiple_of(row * ech, ech), ech)
+        total = epart[pl.ds(first, count), mine, :]
         for d in range(1, rows_n):
-            total = total + ers[d]
-        ered[...] = total
+            total = total + ers[d, pl.ds(first, count)]
+        efull[pl.ds(first, count), mine, :] = total
+        chunk = efull.at[pl.ds(first, count), mine, :]
+
+        def spread(d, carry):
+            there = lax.rem(row + d, rows_n)
+            remote(
+                chunk, chunk, eag_send.at[g], eag_recv.at[g], (core, there, vec)
+            ).start()
+            return carry
+
+        lax.fori_loop(1, rows_n, spread, 0)
         done.wait_send()
-        count = half - 1
-        for d in range(1, half):
-            remote(
-                ered.at[vecs + d - 1], xrecv.at[d - 1], x_send, x_recv,
-                (core, row, lax.rem(vec + vecs - d, vecs)),
-            ).start()
-            remote(
-                ered.at[vecs + count + d - 1], xrecv.at[count + d - 1], x_send, x_recv,
-                (core, row, lax.rem(vec + d, vecs)),
-            ).start()
-        done = remote(xrecv, xrecv, x_send, x_recv, (other, row, vec))
+
+    def margin_gathered(g):
+        first, count = spans[g]
+        view = efull.at[pl.ds(first, count), pl.ds(0, (rows_n - 1) * ech), :]
+        done = remote(view, view, eag_send.at[g], eag_recv.at[g], (other, row, vec))
         done.wait_recv()
         done.wait_send()
-        for d in range(1, half):
-            up = lax.rem(vec + d, vecs)
-            down = lax.rem(vec + vecs - d, vecs)
-            ered[up] = ered[up] + xrecv[d - 1]
-            ered[down] = ered[down] + xrecv[count + d - 1]
-        mine = efull.at[:, pl.ds(row * ech, ech), :]
-        efull[:, pl.ds(row * ech, ech), :] = ered[pl.ds(0, vecs)]
-
-        def spread(d, carry):
-            there = lax.rem(row + d, rows_n)
-            remote(mine, mine, eag_send, eag_recv, (core, there, vec)).start()
-            return carry
-
-        lax.fori_loop(1, rows_n, spread, 0)
-        view = efull.at[:, pl.ds(0, (rows_n - 1) * ech), :]
-        done = remote(view, view, eag_send, eag_recv, (other, row, vec))
-        done.wait_recv()
-        done.wait_send()
-
-    def margins_out():
-        for q in range(vecs):
-            margins_ref[:, q * kept : (q + 1) * kept] = efull[q].T
+
+    def margin_pair(g):
+        first, count = spans[g]
+        span = pl.ds(first, count)
+        return pair_copy(efull.at[span], ein.at[span], 3 + g)
+
+    def margins_out(g):
+        first, count = spans[g]
+        for at in range(first, first + count):
+            away = at if at < half else at - half + 1
+            shift = half if at == vecs - 1 else at if at < half else vecs - away
+            q = lax.rem(vec + shift, vecs)
+            lanes = pl.ds(pl.multiple_of(q * kept, kept), kept)
+            margins_buf[:, lanes] = efull[at].T
+
+    out_copies = [
+        pltpu.make_async_copy(rounded_buf, rounded_ref, out_sem.at[0]),
+        pltpu.make_async_copy(bases_buf, bases_ref, out_sem.at[1]),
+        pltpu.make_async_copy(margins_buf, margins_ref, out_sem.at[2]),
+    ]
 
     bases_scale = math.sqrt(rank)
 
@@ -404,26 +444,47 @@
         gram = full[1]
         yt = fdot(fdot(wt, gram), gram)
         ut = fdot(whiten(yt), yt)
-        bases_ref[...] = ut.T * bases_scale
-        shape_cores(ut)
+        bases_buf[...] = ut.T * bases_scale
+        out_copies[1].start()
+        count = (mh + 2) * kept
         for side in (0, 1):
+            shape_cores(ut, side)
             ring[side, 0, pl.ds(mh * kept, kept), :] = ut[:, :kept]
             ring[side, 0, pl.ds((mh + 1) * kept, kept), :] = ut[:, kept:]
-
-        def env(side, k, q):
+            ring_copy(side, 0, count).start()
+        out_copies[0].start()
+
+        def env(side, k):
             a = ring[side, k, pl.ds(mh * kept, kept), :]
             b = ring[side, k, pl.ds((mh + 1) * kept, kept), :]
             c = ring[0, 0, pl.ds(mh * kept, kept), :]
             d = ring[0, 0, pl.ds((mh + 1) * kept, kept), :]
             return fdot_nt(a, c) + fdot_nt(b, d)
 
-        round_ring((mh + 2) * kept, lambda k: margin_work(k, env))
-        sum_margins()
-        onward = pair_copy(efull, ein, 3)
-        onward.start()
-        margins_out()
-        onward.wait_send()
+        margin_work(0, env)
+        for k in range(1, half):
+            ring_step(k, count)
+            margin_work(k, env)
+        swap_done()
+        margin_scatter(0)
+        margin_gather(0)
+        ring_step(half, count)
+        margin_work(half, env)
+        margin_scatter(1)
+        margin_gathered(0)
+        margin_pair(0).start()
+        margin_gather(1)
+        margins_out(0)
+        margin_gathered(1)
+        margin_pair(1).start()
+        margins_out(1)
+        out_copies[2].start()
+        ring_sent(count)
         to_pair.wait_send()
+        margin_pair(0).wait_send()
+        margin_pair(1).wait_send()
+        for copy in out_copies:
+            copy.wait()
 
     @pl.when(core == 1)
     def back():
@@ -443,15 +504,20 @@
         to_pair.start()
 
         chi, clo = split(full[0])
+        cboth = jnp.concatenate([chi, clo], axis=1)
         part[...] = jnp.zeros_like(part)
 
         def body(i, carry):
-            h = dot(gthi[i], chi) + dot(gthi[i], clo) + dot(gtlo[i], chi)
+            at = pl.ds(pl.multiple_of(i * GROUP * rank, GROUP * rank), GROUP * rank)
+            r = dot(gthi[at, :], cboth)
+            h = r[:, :rank] + r[:, rank:] + dot(gtlo[at, :], chi)
             hi, lo = split(h)
-            part[...] += dot(hi, ghi[i]) + dot(hi, glo[i]) + dot(lo, ghi[i])
-            return carry
-
-        lax.fori_loop(0, modes, body, 0)
+            hi = beside(hi, GROUP)
+            g = ghi[at, :]
+            part[...] += dot(hi, g) + dot(hi, glo[at, :]) + dot(beside(lo, GROUP), g)
+            return carry
+
+        lax.fori_loop(0, modes // GROUP, body, 0)
         sum_rows(1)
         gram = full[1]
         yt = fdot(fdot(xwt, gram), gram)
@@ -469,16 +535,52 @@
         z_pair = pair_copy(zt_ref, zt_ref, 2)
         z_pair.start()
         ut = fdot(kinv, yt)
-        bases_ref[...] = ut.T * bases_scale
-        shape_cores(fdot_nt(ut, low))
-        round_ring(mh * kept, lambda k: None)
-        pair_copy(efull, ein, 3).wait_recv()
-        for k in range(half + 1):
-            margin_work(k, lambda side, k, q: ein[q])
-        sum_margins()
-        margins_out()
+        bases_buf[...] = ut.T * bases_scale
+        out_copies[1].start()
+        ft = fdot_nt(ut, low)
+        count = mh * kept
+        for side in (0, 1):
+            shape_cores(ft, side)
+            ring_copy(side, 0, count).start()
+        out_copies[0].start()
+        for k in range(1, half + 1):
+            ring_step(k, count)
+
+        def env(side, k):
+            return ein[down_at(k) if side == 0 else up_at(k)]
+
+        margin_pair(0).wait_recv()
+        for k in range(1, half):
+            margin_work(k, env)
+        margin_work(0, env)
+        swap_done()
+        margin_scatter(0)
+        margin_pair(1).wait_recv()
+        margin_work(half, env)
+        margin_scatter(1)
+        margin_gather(0)
+        margin_gather(1)
+        margin_gathered(0)
+        margins_out(0)
+        margin_gathered(1)
+        margins_out(1)
+        out_copies[2].start()
+        ring_sent(count)
         to_pair.wait_send()
         z_pair.wait_send()
+        for copy in out_copies:
+            copy.wait()
+
+
+def deliver(*refs):
+    count = (len(refs) - 1) // 2
+    copies = [
+        pltpu.make_async_copy(refs[i], refs[count + i], refs[-1].at[i]) for i in range(count)
+    ]
+    for copy in copies:
+        copy.start()
+    for copy in copies:
+        copy.wait()
 
 
 def build(mesh):
@@ -492,49 +594,61 @@
         mh = modes // 2
         ch = rank // rows_n
         ech = kept // rows_n
-        blocks = vecs + 2 * (half - 1)
         dma = pltpu.SemaphoreType.DMA
         vmem = pl.BlockSpec(memory_space=pltpu.VMEM)
-        rounded, bases, margins = pl.pallas_call(
+        shapes = (
+            jax.ShapeDtypeStruct((kept * modes, kept), F32),
+            jax.ShapeDtypeStruct((rank, kept), F32),
+            jax.ShapeDtypeStruct((kept, vecs * kept), F32),
+        )
+        hbm = pl.BlockSpec(memory_space=pl.ANY)
+        results = pl.pallas_call(
             functools.partial(kernel, (rank, kept, modes, rows_n, vecs)),
-            out_shape=(
-                jax.ShapeDtypeStruct((kept * modes, kept), F32),
-                jax.ShapeDtypeStruct((rank, kept), F32),
-                jax.ShapeDtypeStruct((kept, vecs * kept), F32),
-            ),
-            in_specs=[pl.BlockSpec(memory_space=pl.ANY), vmem, vmem],
-            out_specs=(vmem, vmem, vmem),
+            out_shape=shapes,
+            in_specs=[hbm, vmem, vmem],
+            out_specs=(hbm, hbm, hbm),
             scratch_shapes=[
                 pltpu.VMEM((rank // 128, rank * modes, 128), F32),
-                pltpu.VMEM((modes, rank, rank), BF16),
-                pltpu.VMEM((modes, rank, rank), BF16),
-                pltpu.VMEM((modes, rank, rank), BF16),
-                pltpu.VMEM((modes, rank, rank), BF16),
+                pltpu.VMEM((modes * rank, rank), BF16),
+                pltpu.VMEM((modes * rank, rank), BF16),
+                pltpu.VMEM((modes * rank, rank), BF16),
+                pltpu.VMEM((modes * rank, rank), BF16),
                 pltpu.VMEM((rank, rank), F32),
                 pltpu.VMEM((3, rows_n, ch, rank), F32),
                 pltpu.VMEM((3, rank, rank), F32),
                 pltpu.VMEM((rank, rank), F32),
                 pltpu.VMEM((kept, rank), F32),
                 pltpu.VMEM((kept, kept), F32),
-                pltpu.VMEM((modes, rank, 2 * kept), BF16),
-                pltpu.VMEM((modes, 2 * kept, 2 * kept), BF16),
+                pltpu.VMEM((modes * rank, 2 * kept), BF16),
+                pltpu.VMEM((modes * 2 * kept, 2 * kept), BF16),
                 pltpu.VMEM((2, half + 1, (mh + 2) * kept, kept), F32),
-                pltpu.VMEM((blocks, kept, kept), F32),
-                pltpu.VMEM((rows_n, blocks, ech, kept), F32),
-                pltpu.VMEM((blocks, ech, kept), F32),
-                pltpu.VMEM((2 * (half - 1), ech, kept), F32),
+                pltpu.VMEM((vecs, kept, kept), F32),
+                pltpu.VMEM((rows_n, vecs, ech, kept), F32),
+                pltpu.VMEM((half - 1, 2, kept, kept), F32),
+                pltpu.VMEM((half - 1, 2, kept, kept), F32),
                 pltpu.VMEM((vecs, kept, kept), F32),
                 pltpu.VMEM((vecs, kept, kept), F32),
+                pltpu.VMEM((kept * modes, kept), F32),
+                pltpu.VMEM((rank, kept), F32),
+                pltpu.VMEM((kept, vecs * kept), F32),
                 dma((8, rank // 128)),
                 dma((3,)), dma((3,)), dma((3,)), dma((3,)),
-                dma((4,)), dma((4,)),
+                dma((5,)), dma((5,)),
                 dma((2, half)), dma((2, half)),
-                dma, dma, dma, dma, dma, dma,
+                dma((2,)), dma((2,)), dma((half - 1,)), dma((half - 1,)), dma((2,)), dma((2,)),
+                dma((3,)),
             ],
             compiler_params=pltpu.CompilerParams(
                 collective_id=0, has_side_effects=True, vmem_limit_bytes=58 * 1024 * 1024
             ),
         )(train_cores.reshape(rank * modes, rank), sketch, exit_sketch)
+        rounded, bases, margins = pl.pallas_call(
+            deliver,
+            out_shape=shapes,
+            in_specs=[hbm] * 3,
+            out_specs=(hbm, hbm, hbm),
+            scratch_shapes=[dma((3,))],
+        )(*results)
         return (
             rounded.reshape(1, kept, modes, kept),
             bases[None],

time: 222 us -> 226 us (1.018)
  Pallas kernels: 215 us -> 225 us
  local copies, waits for them, and re-layouts: 5.71 us -> 0 us
    pallas_call x0 -> x1, Pallas kernels: none -> 52.7 us  [local(): pl.pallas_call(deliver, out_shape=shapes, in_specs=[hbm] * 3, out_specs=(...]
    pallas_call x1, Pallas kernels: 215 us -> 173 us  [local(): pl.pallas_call(functools.partial(kernel, (rank, kept, modes, rows_n, vecs...]
    unnamed x3 -> x0, local copies, waits for them, and re-layouts: 5.71 us -> none
where the time goes in v2:
time: 226 us
  Pallas kernels  225 us (100%)
    pallas_call x1, Pallas kernels, local(): pl.pallas_call(functools.partial(kernel, (rank, kept, modes, rows_n, vecs...  173 us
    pallas_call x1, Pallas kernels, local(): pl.pallas_call(deliver, out_shape=shapes, in_specs=[hbm] * 3, out_specs=(...  52.7 us

profile of v2, /device:TPU:1, one launch (start us, length us, event | category | flops | bytes accessed | tf_op | source)
XLA Modules:
  0.0 226.3 jit_solution(9048022160781080996)
XLA Ops:
  0.6 172.7 %shard_map.58 = (f32[2048,128]{1,0:T(8,128)}, f32[256,128]{1,0:T(8,128)}, f32[128,1024]{1,0:T(8,128)}) custom-call(f32[4096,256]{1,0:T(8,128)} %bitcast.4, f32[256,128]{1,0:T(8,128)} %w_ref.1, f32[256,128]{1,0:T(8,128)} %xw_ref.1), custom_call_target="tpu_custom_call" | custom-call | tf_op jit(solution)/shard_map/pallas_call | solution.py:605
  173.3 52.7 %shard_map.59 = (f32[2048,128]{1,0:T(8,128)}, f32[256,128]{1,0:T(8,128)}, f32[128,1024]{1,0:T(8,128)}) custom-call(f32[2048,128]{1,0:T(8,128)} %get-tuple-element.9.refs_0_, f32[256,128]{1,0:T(8,128)} %get-tuple-element.10.refs_1_, f32[128,1024]{1,0:T(8,128)} %get-tuple-element.11.refs_2_), custom_call_target="tpu_custom_call" | custom-call | tf_op jit(solution)/shard_map/pallas_call | solution.py:645

commit v3 on v2

--- a/solution.py
+++ b/solution.py
@@ -103,16 +103,30 @@
     ring, epart, ers, xsend, xrecv, efull, ein, rounded_buf, bases_buf, margins_buf,
     load_sem, rs_send, rs_recv, ag_send, ag_recv, pair_send, pair_recv,
     ring_send, ring_recv, ers_send, ers_recv, x_send, x_recv, eag_send, eag_recv, out_sem,
+    gring, zall, mthi, mtlo, gring_send, gring_recv, z_send, z_recv,
 ):
     rank, kept, modes, rows_n, vecs = sizes
     half = vecs // 2
     mh = modes // 2
     ch = rank // rows_n
     ech = kept // rows_n
+    early = mh // 2
+    sent = mh - early
     core = lax.axis_index("cores")
     row = lax.axis_index("row")
     vec = lax.axis_index("vec")
     other = 1 - core
+
+    side_n = math.isqrt(rows_n)
+    if side_n * side_n == rows_n and side_n > 2:
+        offsets = [(a, b) for a in range(side_n) for b in range(side_n) if a or b]
+        offsets.sort(key=lambda o: -sum(min(v, side_n - v) for v in o))
+        peers = [
+            lax.rem(row // side_n + a, side_n) * side_n + lax.rem(row % side_n + b, side_n)
+            for a, b in offsets
+        ]
+    else:
+        peers = [lax.rem(row + d, rows_n) for d in range(1, rows_n)]
 
     pieces = load_sem.shape[0]
     prow = rank * modes // pieces
@@ -138,15 +152,13 @@
 
     lax.fori_loop(1, rows_n, greet, 0)
     pl.semaphore_signal(barrier, inc=1, device_id=(other, row, vec), device_id_type=MESH)
-    away = sorted({d % vecs for d in range(-(half - 1), half)} | {1, vecs - 1})
-    away = [d for d in away if d != 0]
-    for d in away:
+    for d in range(1, vecs):
         pl.semaphore_signal(
             barrier, inc=1, device_id=(core, row, lax.rem(vec + d, vecs)), device_id_type=MESH
         )
 
     def meet():
-        pl.semaphore_wait(barrier, 2 * (rows_n - 1) + 1 + len(away))
+        pl.semaphore_wait(barrier, 2 * (rows_n - 1) + 1 + vecs - 1)
 
     def remote(src, dst, send, recv, to):
         return pltpu.make_async_remote_copy(
@@ -158,15 +170,14 @@
         return remote(src, dst, pair_send.at[which], pair_recv.at[which], (other, row, vec))
 
     def scatter(which, to_core, first):
-        def send(d, carry):
-            there = lax.rem(row + d, rows_n)
+        slots = [(d + 1, there) for d, there in enumerate(peers)]
+        if first == 0:
+            slots.append((0, row))
+        for d, there in slots:
             remote(
                 part.at[pl.ds(there * ch, ch)], rs.at[which, d],
                 rs_send.at[which], rs_recv.at[which], (to_core, there, vec),
             ).start()
-            return carry
-
-        lax.fori_loop(first, rows_n, send, 0)
 
     def scatter_sent(which, first):
         count = (rows_n - first) * ch
@@ -184,14 +195,10 @@
     def gather(which):
         mine = full.at[which, pl.ds(row * ch, ch)]
 
-        def send(d, carry):
-            there = lax.rem(row + d, rows_n)
+        for there in peers:
             remote(
                 mine, mine, ag_send.at[which], ag_recv.at[which], (core, there, vec)
             ).start()
-            return carry
-
-        lax.fori_loop(1, rows_n, send, 0)
         view = full.at[which, pl.ds(0, (rows_n - 1) * ch)]
         done = remote(view, view, ag_send.at[which], ag_recv.at[which], (other, row, vec))
         done.wait_recv()
@@ -214,6 +221,14 @@
             )
             at = pl.ds(pl.multiple_of(i * rank, rank), rank)
             ghi[at, :], glo[at, :] = split(x)
+            if not with_transposes:
+                place = lax.rem(i, mh) - sent
+
+                @pl.when(place >= 0)
+                def keep():
+                    to = pl.multiple_of(lax.max(place, 0) * rank, rank)
+                    gring[i // mh, 0, pl.ds(to, rank), :] = x
+
             if with_transposes:
                 gthi[at, :], gtlo[at, :] = split(x.T)
             return carry
@@ -262,36 +277,87 @@
                 at = pl.multiple_of(i * 2 * kept, 2 * kept)
                 nw[pl.ds(at, kept), :] = line
                 nw[pl.ds(pl.multiple_of(at + kept, kept), kept), :] = line
-                at = pl.multiple_of((t * group + m) * kept, kept)
+                at = pl.multiple_of((t * group + m + 2) * kept, kept)
                 ring[side, 0, pl.ds(at, kept), :] = n.T
             return carry
 
         lax.fori_loop(0, mh // group, body, 0)
 
-    def ring_copy(side, k, count):
+    def ring_copies(side, k, pieces):
+        to = lax.rem(vec + (1 if side == 0 else vecs - 1), vecs)
+        return [
+            remote(
+                ring.at[side, k, pl.ds(at * kept, count * kept)],
+                ring.at[side, k + 1, pl.ds(at * kept, count * kept)],
+                ring_send.at[side, k, n], ring_recv.at[side, k, n], (core, row, to),
+            )
+            for n, (at, count) in enumerate(pieces)
+        ]
+
+    def ring_step(k, pieces):
+        for n in range(len(pieces)):
+            for side in (0, 1):
+                ring_copies(side, k - 1, pieces)[n].wait_recv()
+                if k < half:
+                    ring_copies(side, k, pieces)[n].start()
+
+    def ring_sent(pieces):
+        for k in range(half):
+            for side in (0, 1):
+                for copy in ring_copies(side, k, pieces):
+                    copy.wait_send()
+
+    def gring_copy(side, k):
         to = lax.rem(vec + (1 if side == 0 else vecs - 1), vecs)
         return remote(
-            ring.at[side, k, pl.ds(0, count)], ring.at[side, k + 1, pl.ds(0, count)],
-            ring_send.at[side, k], ring_recv.at[side, k], (core, row, to),
+            gring.at[side, k], gring.at[side, k + 1],
+            gring_send.at[side, k], gring_recv.at[side, k], (core, row, to),
         )
 
-    def ring_step(k, count):
+    def gring_step(k):
         for side in (0, 1):
             if k > 0:
-                ring_copy(side, k - 1, count).wait_recv()
+                gring_copy(side, k - 1).wait_recv()
             if k < half:
-                ring_copy(side, k, count).start()
-
-    def ring_sent(count):
-        for k in range(half):
-            for side in (0, 1):
-                ring_copy(side, k, count).wait_send()
+                gring_copy(side, k).start()
+
+    def z_copy(d):
+        return remote(
+            zt_ref, zall.at[vecs - d], z_send.at[d], z_recv.at[vecs - d],
+            (core, row, lax.rem(vec + d, vecs)),
+        )
+
+    def z_arrived(d):
+        remote(
+            zall.at[d], zall.at[d], z_send.at[d], z_recv.at[d], (other, row, vec)
+        ).wait_recv()
+
+    def early_maps(k):
+        for side in (0, 1):
+            d = vecs - k if side == 0 else k
+            if side == 0 or d != vecs - k:
+                z_arrived(d)
+            zhi, zlo = split(zall[d])
+            for e in range(early):
+                hi, lo = split(gring[side, k, e * rank : (e + 1) * rank, :])
+                m = dot_nt(zhi, hi) + dot_nt(zhi, lo) + dot_nt(zlo, hi)
+                at = slice(e * kept, (e + 1) * kept)
+                mthi[side, at, :], mtlo[side, at, :] = split(m)
+
+    def early_cores(k):
+        for side in (0, 1):
+            u = jnp.concatenate([ring[side, k, :kept, :], ring[side, k, kept : 2 * kept, :]], 1)
+            uhi, ulo = split(u)
+            m = mthi[side]
+            ring[side, k, (2 + sent) * kept :, :] = (
+                dot_nt(m, uhi) + dot_nt(m, ulo) + dot_nt(mtlo[side], uhi)
+            )
 
     def carry_modes(side, k, et):
         hi, lo = split(et)
         line = jnp.concatenate([hi, lo], axis=1)
         weights = jnp.concatenate([line, line], axis=0)
-        hi, lo = split(ring[side, k, pl.ds(0, mh * kept), :])
+        hi, lo = split(ring[side, k, 2 * kept :, :])
         r = dot(jnp.concatenate([hi, lo], axis=1), weights)
         hi, lo = split(r[:, :kept] + r[:, kept:])
         wide = beside(jnp.concatenate([hi, lo], axis=1), mh)
@@ -339,16 +405,12 @@
     def margin_scatter(g):
         first, count = spans[g]
 
-        def send(d, carry):
-            there = lax.rem(row + d, rows_n)
+        for d, there in enumerate(peers, 1):
             remote(
                 epart.at[pl.ds(first, count), pl.ds(there * ech, ech), :],
                 ers.at[d, pl.ds(first, count)],
                 ers_send.at[g], ers_recv.at[g], (core, there, vec),
             ).start()
-            return carry
-
-        lax.fori_loop(1, rows_n, send, 0)
 
     def margin_gather(g):
         first, count = spans[g]
@@ -362,14 +424,10 @@
         efull[pl.ds(first, count), mine, :] = total
         chunk = efull.at[pl.ds(first, count), mine, :]
 
-        def spread(d, carry):
-            there = lax.rem(row + d, rows_n)
+        for there in peers:
             remote(
                 chunk, chunk, eag_send.at[g], eag_recv.at[g], (core, there, vec)
             ).start()
-            return carry
-
-        lax.fori_loop(1, rows_n, spread, 0)
         done.wait_send()
 
     def margin_gathered(g):
@@ -420,6 +478,7 @@
         meet()
         scatter(0, other, 0)
         by_mode(False)
+        gring_step(0)
         wt = w_ref[...].T
         scatter_sent(0, 0)
 
@@ -427,6 +486,7 @@
         xs[...] = full[0, :kept, :kept]
         eliminate(xs, kept, PANEL)
         kinv, kt = factors(xs, kept)
+        gring_step(1)
         lower_ref[:kept, :kept] = kt.T
         lower_ref[:kept, kept:] = jnp.zeros((kept, rank - kept), F32)
         left = fdot_nt(full[0, kept:, :kept], kinv)
@@ -438,7 +498,11 @@
         to_pair = pair_copy(lower_ref, lower_ref, 1)
         to_pair.start()
 
+        for k in range(2, half):
+            gring_step(k)
         pair_copy(zt_ref, zt_ref, 2).wait_recv()
+        for d in range(1, vecs):
+            z_copy(d).start()
         left_gram(zt_ref[...].T)
         sum_rows(1)
         gram = full[1]
@@ -446,29 +510,36 @@
         ut = fdot(whiten(yt), yt)
         bases_buf[...] = ut.T * bases_scale
         out_copies[1].start()
-        count = (mh + 2) * kept
+        cuts = [(0, 2), (2, sent)]
         for side in (0, 1):
-            shape_cores(ut, side)
-            ring[side, 0, pl.ds(mh * kept, kept), :] = ut[:, :kept]
-            ring[side, 0, pl.ds((mh + 1) * kept, kept), :] = ut[:, kept:]
-            ring_copy(side, 0, count).start()
+            ring[side, 0, :kept, :] = ut[:, :kept]
+            ring[side, 0, kept : 2 * kept, :] = ut[:, kept:]
+            ring_copies(side, 0, cuts)[0].start()
+        for side in (0, 1):
+            shape_cores(ft=ut, side=side)
+            ring_copies(side, 0, cuts)[1].start()
         out_copies[0].start()
+        gring_step(half)
 
         def env(side, k):
-            a = ring[side, k, pl.ds(mh * kept, kept), :]
-            b = ring[side, k, pl.ds((mh + 1) * kept, kept), :]
-            c = ring[0, 0, pl.ds(mh * kept, kept), :]
-            d = ring[0, 0, pl.ds((mh + 1) * kept, kept), :]
+            a = ring[side, k, :kept, :]
+            b = ring[side, k, kept : 2 * kept, :]
+            c = ring[0, 0, :kept, :]
+            d = ring[0, 0, kept : 2 * kept, :]
             return fdot_nt(a, c) + fdot_nt(b, d)
 
         margin_work(0, env)
         for k in range(1, half):
-            ring_step(k, count)
+            early_maps(k)
+            ring_step(k, cuts)
+            early_cores(k)
             margin_work(k, env)
+        early_maps(half)
         swap_done()
         margin_scatter(0)
         margin_gather(0)
-        ring_step(half, count)
+        ring_step(half, cuts)
+        early_cores(half)
         margin_work(half, env)
         margin_scatter(1)
         margin_gathered(0)
@@ -479,7 +550,12 @@
         margin_pair(1).start()
         margins_out(1)
         out_copies[2].start()
-        ring_sent(count)
+        ring_sent(cuts)
+        for d in range(1, vecs):
+            z_copy(d).wait_send()
+        for k in range(half):
+            for side in (0, 1):
+                gring_copy(side, k).wait_send()
         to_pair.wait_send()
         margin_pair(0).wait_send()
         margin_pair(1).wait_send()
@@ -538,13 +614,14 @@
         bases_buf[...] = ut.T * bases_scale
         out_copies[1].start()
         ft = fdot_nt(ut, low)
-        count = mh * kept
+        cuts = [(2, sent), (2 + sent, early)]
         for side in (0, 1):
             shape_cores(ft, side)
-            ring_copy(side, 0, count).start()
+            for copy in ring_copies(side, 0, cuts):
+                copy.start()
         out_copies[0].start()
         for k in range(1, half + 1):
-            ring_step(k, count)
+            ring_step(k, cuts)
 
         def env(side, k):
             return ein[down_at(k) if side == 0 else up_at(k)]
@@ -565,7 +642,7 @@
         margin_gathered(1)
         margins_out(1)
         out_copies[2].start()
-        ring_sent(count)
+        ring_sent(cuts)
         to_pair.wait_send()
         z_pair.wait_send()
         for copy in out_copies:
@@ -573,14 +650,28 @@
 
 
 def deliver(*refs):
-    count = (len(refs) - 1) // 2
-    copies = [
-        pltpu.make_async_copy(refs[i], refs[count + i], refs[-1].at[i]) for i in range(count)
+    sources, targets, buffers = refs[:3], refs[3:6], refs[6:9]
+    into, out = refs[9:]
+    spans = [
+        (n, pl.ds(t * (src.shape[0] // count), src.shape[0] // count))
+        for n, (src, count) in enumerate(zip(sources, (4, 1, 2)))
+        for t in range(count)
     ]
-    for copy in copies:
+    loads = [
+        pltpu.make_async_copy(sources[n].at[span], buffers[n].at[span], into.at[t])
+        for t, (n, span) in enumerate(spans)
+    ]
+    stores = [
+        pltpu.make_async_copy(buffers[n].at[span], targets[n].at[span], out.at[t])
+        for t, (n, span) in enumerate(spans)
+    ]
+    for copy in loads:
         copy.start()
-    for copy in copies:
-        copy.wait()
+    for load, store in zip(loads, stores):
+        load.wait()
+        store.start()
+    for store in stores:
+        store.wait()
 
 
 def build(mesh):
@@ -592,6 +683,7 @@
         kept = sketch.shape[1]
         half = vecs // 2
         mh = modes // 2
+        early = mh // 2
         ch = rank // rows_n
         ech = kept // rows_n
         dma = pltpu.SemaphoreType.DMA
@@ -634,9 +726,14 @@
                 dma((8, rank // 128)),
                 dma((3,)), dma((3,)), dma((3,)), dma((3,)),
                 dma((5,)), dma((5,)),
-                dma((2, half)), dma((2, half)),
+                dma((2, half, 2)), dma((2, half, 2)),
                 dma((2,)), dma((2,)), dma((half - 1,)), dma((half - 1,)), dma((2,)), dma((2,)),
                 dma((3,)),
+                pltpu.VMEM((2, half + 1, early * rank, rank), F32),
+                pltpu.VMEM((vecs, kept, rank), F32),
+                pltpu.VMEM((2, early * kept, rank), BF16),
+                pltpu.VMEM((2, early * kept, rank), BF16),
+                dma((2, half)), dma((2, half)), dma((vecs,)), dma((vecs,)),
             ],
             compiler_params=pltpu.CompilerParams(
                 collective_id=0, has_side_effects=True, vmem_limit_bytes=58 * 1024 * 1024
@@ -647,7 +744,7 @@
             out_shape=shapes,
             in_specs=[hbm] * 3,
             out_specs=(hbm, hbm, hbm),
-            scratch_shapes=[dma((3,))],
+            scratch_shapes=[pltpu.VMEM(x.shape, F32) for x in shapes] + [dma((7,)), dma((7,))],
         )(*results)
         return (
             rounded.reshape(1, kept, modes, kept),

time: 226 us -> 165 us (0.73)
  Pallas kernels: 225 us -> 164 us
    pallas_call x1, Pallas kernels: 52.7 us -> 2.25 us  [local(): pl.pallas_call(deliver, out_shape=shapes, in_specs=[hbm] * 3, out_specs=(...]
    pallas_call x1, Pallas kernels: 173 us -> 162 us  [local(): pl.pallas_call(functools.partial(kernel, (rank, kept, modes, rows_n, vecs...]
where the time goes in v3:
time: 165 us
  Pallas kernels  164 us (99%)
    pallas_call x1, Pallas kernels, local(): pl.pallas_call(functools.partial(kernel, (rank, kept, modes, rows_n, vecs...  162 us

profile of v3, /device:TPU:1, one launch (start us, length us, event | category | flops | bytes accessed | tf_op | source)
XLA Modules:
  0.0 164.7 jit_solution(16803661972846654216)
XLA Ops:
  0.6 161.6 %shard_map.58 = (f32[2048,128]{1,0:T(8,128)}, f32[256,128]{1,0:T(8,128)}, f32[128,1024]{1,0:T(8,128)}) custom-call(f32[4096,256]{1,0:T(8,128)} %bitcast.4, f32[256,128]{1,0:T(8,128)} %w_ref.1, f32[256,128]{1,0:T(8,128)} %xw_ref.1), custom_call_target="tpu_custom_call" | custom-call | tf_op jit(solution)/shard_map/pallas_call | solution.py:697
  162.3 2.2 %shard_map.59 = (f32[2048,128]{1,0:T(8,128)}, f32[256,128]{1,0:T(8,128)}, f32[128,1024]{1,0:T(8,128)}) custom-call(f32[2048,128]{1,0:T(8,128)} %get-tuple-element.9.refs_0_, f32[256,128]{1,0:T(8,128)} %get-tuple-element.10.refs_1_, f32[128,1024]{1,0:T(8,128)} %get-tuple-element.11.refs_2_), custom_call_target="tpu_custom_call" | custom-call | tf_op jit(solution)/shard_map/pallas_call | solution.py:742
